TPU v7x, 128 devices: a whole 4x4x4 slice. The times are simulated.
128 devices in a mesh: surf: 32 (over z, y, core), vol: 4 (over x).
Axes of the slice: x: 4, y: 4, z: 4, core: 2. Of those that a mesh axis runs over, the one named last changes fastest.
Arguments:
- casting: bfloat16 [131072, 128], P(('surf', 'vol')), may hold values from -5 to 5, as said below
- owner: int32 [131072, 1], P(('surf', 'vol')), may hold values from 0 to 127; in each aligned block of 1024 rows (0 to 1023, 1024 to 2047, ...) at most 32 rows name the same one
- face_id: int32 [131072], P(('surf', 'vol')), may hold values from 0 to 2047
- mold_faces: bfloat16 [262144, 128], P(('surf', 'vol')), may hold values from -5 to 5, as said below
- mortar_d: bfloat16 [64, 64], replicated, may hold values from -0.75 to 0.75
- mortar_m: bfloat16 [64, 64], replicated, may hold values from -0.75 to 0.75
- conduct: bfloat16 [128, 128], replicated, may hold values from -0.5 to 0.5
- volume: bfloat16 [262144, 128], P(('surf', 'vol')), may hold values from -6 to 6
Outputs:
- casting_out: bfloat16 [131072, 128], P(('surf', 'vol'))
- mold_out: bfloat16 [262144, 128], P(('surf', 'vol'))
Inputs may be any that keep to these rules, and one draw needn't show every extreme that they name: Among the 1024 rows of one device no owner is named more than 32 times, a bound that some block reaches. `casting`: temperatures lie within -5 to 5; conductances lie within 0.3 to 3. `mold_faces`: temperatures lie within -5 to 5; area weights lie within 0.3 to 3.
All inputs are finite; a program needn't handle non-finite values.
Results may differ from a plain program's by a relative error of at most 0.0055.
Values may be sent and summed in bfloat16 or wider, within the bound.
A program may use at most 64 MiB of HBM per device.

v0:
```python
import math

import jax
import jax.numpy as jnp
from jax import lax
from jax.sharding import PartitionSpec as P

relax = 0.5


def contact(rows, mold_rows, stacked, joined, node_count):
    pair_rows = jnp.concatenate([rows[:, :node_count], mold_rows[:, :node_count]], axis=1)
    gap_jump = jnp.dot(pair_rows, stacked, preferred_element_type=jnp.float32)
    heat_flux = (
        rows[:, node_count:].astype(jnp.float32)
        * mold_rows[:, node_count:].astype(jnp.float32)
        * gap_jump
    ).astype(jnp.bfloat16)
    projected = jnp.dot(heat_flux, joined, preferred_element_type=jnp.float32)
    answer = jnp.concatenate([projected[:, :node_count], gap_jump], axis=1).astype(jnp.bfloat16)
    gained = projected[:, node_count:].astype(jnp.bfloat16)
    return (answer, gained)


def local(casting, owner, face_id, mold_faces, mortar_d, mortar_m, conduct, volume):
    seg_rows, row_width = casting.shape
    node_count = mortar_d.shape[0]
    face_rows = mold_faces.shape[0]
    surf_count = lax.axis_size("surf")
    vol_count = lax.axis_size("vol")
    devices = surf_count * vol_count
    capacity = 4 * seg_rows // devices
    slots = devices * capacity
    target = owner[:, 0]
    hits = (target[:, None] == jnp.arange(devices, dtype=jnp.int32)[None, :]).astype(jnp.int32)
    position = jnp.sum((jnp.cumsum(hits, axis=0) - 1) * hits, axis=1)
    slot_index = target * capacity + position
    send_ids = jnp.full((slots,), -1, jnp.int32).at[slot_index].set(face_id)
    block_rows = math.gcd(512, slots)
    turns = slots // block_rows
    stacked = jnp.concatenate([mortar_d.T, -mortar_m.T], axis=0)
    joined = jnp.concatenate([mortar_d, mortar_m], axis=1)
    face_range = jnp.arange(face_rows, dtype=jnp.int32)
    send_rows = jnp.zeros((slots, row_width), jnp.bfloat16).at[slot_index].set(casting)
    got_rows, got_ids = (
        lax.all_to_all(
            send_rows.reshape(devices, capacity, row_width),
            ("surf", "vol"),
            split_axis=0,
            concat_axis=0,
            tiled=True,
        ),
        lax.all_to_all(
            send_ids.reshape(devices, capacity),
            ("surf", "vol"),
            split_axis=0,
            concat_axis=0,
            tiled=True,
        ),
    )
    flat_rows = got_rows.reshape(turns, block_rows, row_width)
    flat_ids = got_ids.reshape(turns, block_rows)

    def settle(totals, pieces):
        rows, row_ids = pieces
        selector = (row_ids[:, None] == face_range[None, :]).astype(jnp.bfloat16)
        mold_rows = jnp.dot(selector, mold_faces, preferred_element_type=jnp.float32).astype(
            jnp.bfloat16
        )
        answer, gained = contact(rows, mold_rows, stacked, joined, node_count)
        totals = totals + lax.dot_general(
            selector, gained, (((0,), (0,)), ((), ())), preferred_element_type=jnp.float32
        )
        return (totals, answer)

    totals, answers = lax.scan(
        settle, jnp.zeros((face_rows, node_count), jnp.float32), (flat_rows, flat_ids)
    )
    returned = lax.all_to_all(
        answers.reshape(devices, capacity, row_width),
        ("surf", "vol"),
        split_axis=0,
        concat_axis=0,
        tiled=True,
    )
    casting_out = returned.reshape(slots, row_width)[slot_index]
    face_totals = totals.astype(jnp.bfloat16)
    quarter = face_rows // vol_count
    relaid = lax.all_to_all(
        face_totals.reshape(vol_count, quarter * node_count // row_width, row_width),
        "vol",
        split_axis=0,
        concat_axis=0,
        tiled=True,
    )
    heat = jnp.dot(volume, conduct, preferred_element_type=jnp.float32)
    placed = relaid.reshape(face_rows, node_count).astype(jnp.float32)
    inject = jnp.concatenate([placed, jnp.zeros((face_rows, node_count), jnp.float32)], axis=1)
    mold_out = (volume.astype(jnp.float32) + relax * (inject - heat)).astype(jnp.bfloat16)
    return (casting_out, mold_out)


def solution(mesh):
    return jax.shard_map(
        local,
        mesh=mesh,
        in_specs=(
            P(("surf", "vol"), None),
            P(("surf", "vol"), None),
            P(("surf", "vol")),
            P(("surf", "vol"), None),
            P(),
            P(),
            P(),
            P(("surf", "vol"), None),
        ),
        out_specs=(P(("surf", "vol"), None), P(("surf", "vol"), None)),
        check_vma=False,
    )
```

profile of v0, /device:TPU:1, one launch (start us, length us, event | category | flops | bytes accessed | tf_op | source)
XLA Modules:
  0.0 120.3 jit_solution(93729381224445039)
XLA Ops:
  0.6 0.8 copy.20
  1.9 0.5 copy-done.4
  2.4 0.4 fusion.19
  2.8 4.5 %scatter_custom_fusion = s32[4096]{0:T(1024)S(1)} fusion(s32[1024]{0:T(1024)S(1)} %bitcast.57, s32[1024]{0:T(1024)} %param.12, s32[]{:T(128)} %constant.20.clone.1), kind=kCustom, calls=%fused_computation.45 | custom fusion | bytes 16896 | tf_op jit(solution)/shard_map/scatter | solution.py:38
  7.3 0.7 all_to_all.15
  8.0 11.5 %all-to-all-start = ((s32[128,1,32]{2,1,0:T(1,128)}), s32[128,1,32]{2,1,0:T(1,128)S(1)}, u32[]{:S(2)}, u32[]{:S(2)}) async-start(s32[128,1,32]{2,1,0:T(1,128)} %bitcast.7), calls=%async_computation | async-start | bytes 131072 | tf_op jit(solution)/shard_map/all_to_all | solution.py:53
  19.5 4.7 %scatter_custom_fusion.1 = bf16[4096,128]{1,0:T(8,128)(2,1)} fusion(s32[1024]{0:T(1024)S(1)} %bitcast.58, bf16[1024,128]{1,0:T(8,128)(2,1)} %param.10, bf16[]{:T(256)} %constant.15.clone.1), kind=kCustom, calls=%fused_computation.33 | custom fusion | bytes 1049088 | tf_op jit(solution)/shard_map/scatter | solution.py:44
  24.2 4.9 %all-to-all-done = s32[128,1,32]{2,1,0:T(1,128)S(1)} async-done(((s32[128,1,32]{2,1,0:T(1,128)}), s32[128,1,32]{2,1,0:T(1,128)S(1)}, u32[]{:S(2)}, u32[]{:S(2)}) %all-to-all-start) | async-done | bytes 16416 | tf_op jit(solution)/shard_map/all_to_all | solution.py:53
  29.1 4.8 %all-to-all-start.1 = ((bf16[128,32,128]{2,1,0:T(8,128)(2,1)}), bf16[128,32,128]{2,1,0:T(8,128)(2,1)S(1)}, u32[]{:S(2)}, u32[]{:S(2)}) async-start(bf16[128,32,128]{2,1,0:T(8,128)(2,1)} %bitcast.8), calls=%async_computation.1 | async-start | bytes 2097152 | tf_op jit(solution)/shard_map/all_to_all | solution.py:46
  34.3 0.5 broadcast.60
  34.8 0.8 reduce.3
  35.7 17.8 %all-to-all-done.1 = bf16[128,32,128]{2,1,0:T(8,128)(2,1)S(1)} async-done(((bf16[128,32,128]{2,1,0:T(8,128)(2,1)}), bf16[128,32,128]{2,1,0:T(8,128)(2,1)S(1)}, u32[]{:S(2)}, u32[]{:S(2)}) %all-to-all-start.1) | async-done | bytes 1048608 | tf_op jit(solution)/shard_map/all_to_all | solution.py:46
  53.5 28.5 %while.13 = (s32[]{:T(128)}, f32[2048,64]{0,1:T(8,128)S(1)}, bf16[8,512,128]{2,1,0:T(8,128)(2,1)}, s32[8,512]{1,0:T(8,128)S(1)}, bf16[8,512,128]{2,1,0:T(8,128)(...) while((s32[]{:T(128)}, f32[2048,64]{0,1:T(8,128)S(1)}, ...), condition=%wide.region_6.7_spmd.clone, body=%wide.region_5.6_spmd.clone.sunk | while | flops 422641664 | bytes 4366467 | solution.py:76
  53.6 1.1 fusion.45
  55.0 0.2 convolution_convert_fusion.2
  55.4 1.0 fusion.47
  56.4 0.7 constant_dynamic-update-slice_fusion.2
  57.1 1.1 fusion.45
  58.6 0.2 convolution_convert_fusion.2
  59.0 1.0 fusion.47
  60.0 0.7 constant_dynamic-update-slice_fusion.2
  60.7 1.1 fusion.45
  62.6 1.0 fusion.47
  63.6 0.7 constant_dynamic-update-slice_fusion.2
  64.3 1.1 fusion.45
  66.1 1.0 fusion.47
  67.2 0.7 constant_dynamic-update-slice_fusion.2
  67.8 1.1 fusion.45
  69.7 1.0 fusion.47
  70.7 0.7 constant_dynamic-update-slice_fusion.2
  71.4 1.1 fusion.45
  72.8 0.2 convolution_convert_fusion.2
  73.3 1.0 fusion.47
  74.3 0.7 constant_dynamic-update-slice_fusion.2
  74.9 1.1 fusion.45
  76.8 1.0 fusion.47
  77.8 0.7 constant_dynamic-update-slice_fusion.2
  78.5 1.1 fusion.45
  80.4 1.0 fusion.47
  81.4 0.7 constant_dynamic-update-slice_fusion.2
  82.1 0.3 copy.27
  82.4 0.3 reshape.89
  82.7 8.6 %all_to_all.24 = bf16[4,256,128]{2,1,0:T(8,128)(2,1)S(1)} all-to-all(bf16[4,256,128]{2,1,0:T(8,128)(2,1)S(1)} %reshape.89), channel_id=1, replica_groups=mesh['surf'=32,'vol'=4] {'vol'}, dimensions={0} | all-to-all | bytes 524288 | tf_op jit(solution)/shard_map/all_to_all | solution.py:89
  91.3 4.9 %all-to-all-start.2 = ((bf16[128,32,128]{2,1,0:T(8,128)(2,1)}), bf16[128,32,128]{2,1,0:T(8,128)(2,1)S(1)}, u32[]{:S(2)}, u32[]{:S(2)}) async-start(bf16[128,32,128]{2,1,0:T(8,128)(2,1)} %bitcast.12), calls=%async_computation.2 | async-start | bytes 2097152 | tf_op jit(solution)/shard_map/all_to_all | solution.py:79
  96.2 0.2 convert_element_type.43
  96.5 1.1 fusion.18
  97.6 18.3 %all-to-all-done.2 = bf16[128,32,128]{2,1,0:T(8,128)(2,1)S(1)} async-done(((bf16[128,32,128]{2,1,0:T(8,128)(2,1)}), bf16[128,32,128]{2,1,0:T(8,128)(2,1)S(1)}, u32[]{:S(2)}, u32[]{:S(2)}) %all-to-all-start.2) | async-done | bytes 1048608 | tf_op jit(solution)/shard_map/all_to_all | solution.py:79
  116.0 4.3 %gather_fusion = bf16[1024,128]{1,0:T(8,128)(2,1)} fusion(bf16[4096,128]{1,0:T(8,128)(2,1)S(1)} %bitcast.49, s32[1024]{0:T(1024)S(1)} %broadcast_clamp_fusion), kind=kCustom, calls=%fused_computation | custom fusion | bytes 528384 | tf_op jit(solution)/shard_map/gather | solution.py:86
  (113 shorter events, 6.0 us)
Async XLA Ops:
  0.6 95.9 %copy-start = (bf16[128,128]{1,0:T(8,128)(2,1)S(1)}, bf16[128,128]{1,0:T(8,128)(2,1)}, u32[]{:S(2)}) copy-start(bf16[128,128]{1,0:T(8,128)(2,1)} %param.16) | copy-start | bytes 98308
  1.7 0.7 copy-start.4
  8.0 21.1 %all-to-all-start = ((s32[128,1,32]{2,1,0:T(1,128)}), s32[128,1,32]{2,1,0:T(1,128)S(1)}, u32[]{:S(2)}, u32[]{:S(2)}) async-start(s32[128,1,32]{2,1,0:T(1,128)} %bitcast.7), calls=%async_computation | async-start | bytes 131072 | tf_op jit(solution)/shard_map/all_to_all | solution.py:53
  29.1 4.9 %copy-start.3 = (bf16[64,64]{1,0:T(8,128)(2,1)S(1)}, bf16[64,64]{1,0:T(8,128)(2,1)}, u32[]{:S(2)}) copy-start(bf16[64,64]{1,0:T(8,128)(2,1)} %param.14) | copy-start | bytes 24580
  29.1 5.0 %copy-start.2 = (bf16[64,64]{1,0:T(8,128)(2,1)S(1)}, bf16[64,64]{1,0:T(8,128)(2,1)}, u32[]{:S(2)}) copy-start(bf16[64,64]{1,0:T(8,128)(2,1)} %param.15) | copy-start | bytes 24580
  29.1 24.5 %copy-start.5 = (bf16[2048,128]{1,0:T(8,128)(2,1)S(1)}, bf16[2048,128]{1,0:T(8,128)(2,1)}, u32[]{:S(2)}) copy-start(bf16[2048,128]{1,0:T(8,128)(2,1)} %param.13) | copy-start | bytes 1572868
  29.1 24.4 %all-to-all-start.1 = ((bf16[128,32,128]{2,1,0:T(8,128)(2,1)}), bf16[128,32,128]{2,1,0:T(8,128)(2,1)S(1)}, u32[]{:S(2)}, u32[]{:S(2)}) async-start(bf16[128,32,128]{2,1,0:T(8,128)(2,1)} %bitcast.8), calls=%async_computation.1 | async-start | bytes 2097152 | tf_op jit(solution)/shard_map/all_to_all | solution.py:46
  91.3 5.2 %copy-start.1 = (bf16[2048,128]{1,0:T(8,128)(2,1)S(1)}, bf16[2048,128]{1,0:T(8,128)(2,1)}, u32[]{:S(2)}) copy-start(bf16[2048,128]{1,0:T(8,128)(2,1)} %param.17) | copy-start | bytes 1572868
  91.3 24.7 %all-to-all-start.2 = ((bf16[128,32,128]{2,1,0:T(8,128)(2,1)}), bf16[128,32,128]{2,1,0:T(8,128)(2,1)S(1)}, u32[]{:S(2)}, u32[]{:S(2)}) async-start(bf16[128,32,128]{2,1,0:T(8,128)(2,1)} %bitcast.12), calls=%async_computation.2 | async-start | bytes 2097152 | tf_op jit(solution)/shard_map/all_to_all | solution.py:79
where the time goes:
time: 121 us; the launch traced here: 120 us
  waiting for transfers between devices  41.1 us (34%)
  local copies, waits for them, and re-layouts  24.7 us (20%)
  starting transfers between devices  21.3 us (18%)
  matrix products  21.3 us (18%)
  blocking collectives  8.62 us (7%)
  other arithmetic  1.76 us (1%)
    all_to_all x1, waiting for transfers between devices, local(): lax.all_to_all(answers.reshape(devices, capacity, row_width), ('surf', 'v...  18.3 us
    all_to_all x1, waiting for transfers between devices, local(): lax.all_to_all(send_rows.reshape(devices, capacity, row_width), ('surf',...  17.8 us
    all_to_all x1, starting transfers between devices, local(): lax.all_to_all(send_ids.reshape(devices, capacity), ('surf', 'vol'), spli...  11.5 us
    all_to_all x1, blocking collectives, local(): lax.all_to_all(face_totals.reshape(vol_count, quarter * node_count // row...  8.62 us
    dot_general x8, matrix products, settle(): jnp.dot(selector, mold_faces, preferred_element_type=jnp.float32)  8.6 us
    dot_general x8, matrix products, settle(): lax.dot_general(selector, gained, (((0,), (0,)), ((), ())), preferred_ele...  8.09 us
    dynamic_update_slice x16, local copies, waits for them, and re-layouts, local(): lax.scan(settle, jnp.zeros((face_rows, node_count), jnp.float32), (flat_r...  6.25 us
    all_to_all x1, starting transfers between devices, local(): lax.all_to_all(answers.reshape(devices, capacity, row_width), ('surf', 'v...  4.94 us
  transfers between devices with their start and end apart: 3, of which 3 were waited for; matrix products, arithmetic and copies ran while one was open for 6% of the time, Pallas kernels for 0%

commit v1 on v0

v1 whole, which is shorter than its diff:
```python
import functools

import jax
import jax.numpy as jnp
from jax import lax
from jax.experimental import pallas as pl
from jax.experimental.pallas import tpu as pltpu
from jax.sharding import PartitionSpec as P

MESH = pl.DeviceIdType.MESH
BF = jnp.bfloat16
F32 = jnp.float32
I32 = jnp.int32

PEERS = 128
PER = 32
BATCH = 16
BATCHES = PEERS // BATCH
SLOTS = BATCH * PER
NODES = 64
ROW = 128
SEGS = 1024
FACES = 2048
QUARTER = FACES // 4


def iota(shape, dim):
    return lax.broadcasted_iota(I32, shape, dim)


def kernel(
    owner_ref,
    face_ref,
    d_ref,
    m_ref,
    conduct_ref,
    casting_hbm,
    mold_hbm,
    volume_hbm,
    cout_hbm,
    mout_hbm,
    casting_v,
    mold_v,
    volume_v,
    send_v,
    recv_v,
    ans_v,
    back_v,
    ids_send,
    ids_recv,
    wgap_v,
    mfour_v,
    wcond_v,
    tile_v,
    spread_v,
    row8_v,
    slotrep_v,
    totals_v,
    quarter_v,
    placed_v,
    acc_v,
    cout_v,
    mout_v,
    load_sem,
    out_sem,
    row_sem,
    id_sem,
    ans_sem,
    tot_sem,
    sent_sem,
):
    surf = lax.axis_index("surf")
    x = lax.axis_index("vol")
    z, y, c = surf // 8, lax.rem(surf // 2, 4), lax.rem(surf, 2)

    def peer(g, i, sign):
        dz, dy = i // 4, i % 4
        pz = lax.rem(z + 4 + sign * dz, 4)
        py = lax.rem(y + 4 + sign * dy, 4)
        px = lax.rem(x + 16 + sign * (g // 2 + dz + dy), 4)
        pc = lax.rem(c + lax.rem(g, 2) + dz, 2)
        return (pz * 8 + py * 2 + pc, px)

    def each_peer(g, act, own):
        for i in range(BATCH):
            if i == 0:
                pl.when(g > 0)(functools.partial(act, g, i))
                if own is not None:
                    pl.when(g == 0)(own)
            else:
                act(g, i)

    loads = [
        pltpu.make_async_copy(casting_hbm, casting_v, load_sem.at[0]),
        pltpu.make_async_copy(mold_hbm.at[pl.ds(0, 1024)], mold_v.at[:, pl.ds(0, ROW)], load_sem.at[1]),
        pltpu.make_async_copy(mold_hbm.at[pl.ds(1024, 1024)], mold_v.at[:, pl.ds(ROW, ROW)], load_sem.at[2]),
        pltpu.make_async_copy(volume_hbm, volume_v, load_sem.at[3]),
    ]
    for load in loads:
        load.start()

    barrier = pltpu.get_barrier_semaphore()

    def greet(g, _):
        def one(g, i):
            pl.semaphore_signal(barrier, inc=1, device_id=peer(g, i, 1), device_id_type=MESH)

        each_peer(g, one, None)
        return 0

    lax.fori_loop(0, BATCHES, greet, 0)

    owner = owner_ref[...]
    dx = (owner & 3) - x & 3
    dc = (owner >> 2 & 1) - c & 1
    dy = (owner >> 3 & 3) - y & 3
    dz = (owner >> 5 & 3) - z & 3
    order = (dx - dz - dy & 3) * 32 + (dc - dz & 1) * 16 + dz * 4 + dy
    down, lane = iota((ROW, ROW), 0), iota((ROW, ROW), 1)
    before = jnp.concatenate([(down < lane).astype(F32), jnp.ones((ROW, ROW), F32)], axis=1).astype(BF)
    hits, sofar = [], jnp.zeros((PEERS, ROW), F32)
    for b in range(8):
        hit = down == order[b : b + 1, :]
        hits.append(hit.astype(F32).astype(BF))
        count = jnp.dot(hits[b], before, preferred_element_type=F32)
        rank = jnp.sum(jnp.where(hit, count[:, :ROW] + sofar, 0.0), axis=0, keepdims=True)
        sofar = sofar + count[:, ROW:]
        row8_v[b : b + 1, :] = rank
    slot8 = (order * PER).astype(F32) + row8_v[...]
    row8_v[...] = slot8
    slot_t = slot8.T
    face_t = face_ref[...].astype(F32).T
    table = jnp.zeros((PEERS, ROW), F32)
    for b in range(8):
        slot = jnp.broadcast_to(slot_t[:, b : b + 1], (ROW, ROW)).astype(I32)
        face = jnp.broadcast_to(face_t[:, b : b + 1], (ROW, ROW)).astype(I32)
        slotrep_v[pl.ds(b * ROW, ROW), :] = slot
        part = jnp.where(lane < 32, face & 255, jnp.where(lane < 64, face >> 8 & 3, face >> 10))
        part = jnp.where(((lane & 31) == (slot & 31)) & (lane < 96), part, 0)
        table = table + jnp.dot(hits[b], part.astype(F32).astype(BF), preferred_element_type=F32)
    ids_send[...] = table

    wgap_v[...] = jnp.zeros_like(wgap_v)
    wgap_v[NODES:, 0:NODES] = d_ref[...]
    wgap_v[NODES:, ROW : ROW + NODES] = -m_ref[...]
    mtwo = jnp.concatenate([m_ref[...], m_ref[...]], axis=1)
    mfour_v[...] = jnp.zeros_like(mfour_v)
    mfour_v[NODES:, 0:ROW] = mtwo
    mfour_v[NODES:, ROW:] = mtwo
    for half in range(2):
        pick = jnp.where((down == lane + half * NODES) & (lane < NODES), 0.5, 0.0)
        wcond_v[half, 0:ROW, :] = pick.astype(BF)
        wcond_v[half, ROW:, :] = (conduct_ref[...].astype(F32) * -0.5).astype(BF)
    wide_d, wide_l = iota((ROW, SLOTS), 0), iota((ROW, SLOTS), 1)
    tile = jnp.where(wide_d == (wide_l & 31), 1.0, jnp.where(wide_d == (wide_l & 31) + 64, 256.0, 0.0))
    tile_v[...] = tile.astype(BF)
    down2, lane2 = iota((ROW, 2 * ROW), 0), iota((ROW, 2 * ROW), 1)
    part2 = down2 >> 5
    spread = jnp.where(
        lane2 < ROW,
        jnp.where(part2 == 0, 1.0, jnp.where(part2 == 1, 256.0, 0.0)),
        jnp.where(part2 == 1, 1.0, jnp.where(part2 == 2, 4.0, 0.0)),
    )
    spread_v[...] = spread.astype(BF)
    totals_v[...] = jnp.zeros_like(totals_v)
    acc_v[...] = jnp.zeros_like(acc_v)

    loads[0].wait()

    def pack(g, _):
        want = iota((SLOTS, ROW), 0) + g * SLOTS
        want = want.astype(F32)
        pick = jnp.concatenate(
            [(want == row8_v[b : b + 1, :]).astype(F32).astype(BF) for b in range(8)], axis=1
        )
        rows = jnp.dot(pick, casting_v[...], preferred_element_type=F32).astype(BF)
        send_v[pl.ds(g * BATCH, BATCH)] = rows.reshape(BATCH, PER, ROW)
        return 0

    lax.fori_loop(0, BATCHES, pack, 0)
    pl.semaphore_wait(barrier, PEERS - 1)

    def send(g, _):
        def one(g, i):
            j = g * BATCH + i
            to = peer(g, i, 1)
            pltpu.make_async_remote_copy(
                src_ref=ids_send.at[pl.ds(j, 1)],
                dst_ref=ids_recv.at[pl.ds(j, 1)],
                send_sem=sent_sem.at[0],
                recv_sem=id_sem.at[g],
                device_id=to,
                device_id_type=MESH,
            ).start()
            pltpu.make_async_remote_copy(
                src_ref=send_v.at[j],
                dst_ref=recv_v.at[j],
                send_sem=sent_sem.at[1],
                recv_sem=row_sem.at[g],
                device_id=to,
                device_id_type=MESH,
            ).start()

        def own():
            pltpu.make_async_copy(ids_send.at[pl.ds(0, 1)], ids_recv.at[pl.ds(0, 1)], id_sem.at[0]).start()
            pltpu.make_async_copy(send_v.at[0], recv_v.at[0], row_sem.at[0]).start()

        each_peer(g, one, own)
        return 0

    lax.fori_loop(0, BATCHES, send, 0)
    loads[1].wait()
    loads[2].wait()

    def wait_for(ref, sem):
        pltpu.make_async_copy(ref, ref, sem).wait()

    def settle(g, _):
        span = pl.ds(pl.multiple_of(g * BATCH, BATCH), BATCH)
        wait_for(ids_recv.at[span], id_sem.at[g])
        wait_for(recv_v.at[span], row_sem.at[g])
        ids = ids_recv[span, :]
        across = jnp.dot(ids.astype(BF), tile_v[...], preferred_element_type=F32)
        mine = iota((BATCH, SLOTS), 0) == iota((BATCH, SLOTS), 1) >> 5
        across = jnp.sum(jnp.where(mine, across, 0.0), axis=0, keepdims=True)
        keep = iota((PER, ROW), 0) == (iota((PER, ROW), 1) & 31)
        spaced = jnp.where(keep[None], jnp.broadcast_to(ids[:, None, :], (BATCH, PER, ROW)), 0.0)
        spaced = spaced.reshape(SLOTS, ROW).astype(BF)
        both = jnp.dot(spaced, spread_v[...], preferred_element_type=F32)
        low, high = both[:, :ROW], both[:, ROW:]
        lanes = iota((SLOTS, ROW), 1).astype(F32)
        pick = jnp.concatenate([(low - t * ROW == lanes).astype(F32).astype(BF) for t in range(8)], axis=1)
        found = jnp.dot(pick, mold_v[...], preferred_element_type=F32)
        upper = high >= 4.0
        faces = jnp.where(upper, found[:, ROW:], found[:, :ROW]).astype(BF)
        rows = recv_v[span].reshape(SLOTS, ROW)
        pair = jnp.concatenate([rows, faces], axis=1)
        gap = lax.dot_general(pair, wgap_v[...], (((1,), (1,)), ((), ())), preferred_element_type=F32)
        flux = (rows.astype(F32) * faces.astype(F32) * gap).astype(BF)
        back = jnp.dot(flux, wgap_v[:, :ROW], preferred_element_type=F32)
        answer = (back + gap).astype(BF)
        ans_v[span] = answer.reshape(BATCH, PER, ROW)

        def one(g, i):
            j = g * BATCH + i
            pltpu.make_async_remote_copy(
                src_ref=ans_v.at[j],
                dst_ref=back_v.at[j],
                send_sem=sent_sem.at[2],
                recv_sem=ans_sem.at[g],
                device_id=peer(g, i, -1),
                device_id_type=MESH,
            ).start()

        def own():
            pltpu.make_async_copy(ans_v.at[0], back_v.at[0], ans_sem.at[0]).start()

        each_peer(g, one, own)
        gain = jnp.dot(flux, mfour_v[...], preferred_element_type=F32)
        column = jnp.where(upper, high - 4.0, high)
        block = (iota((SLOTS, ROW), 1) >> 6).astype(F32)
        gain = jnp.concatenate(
            [
                jnp.where(column == block, gain[:, :ROW], 0.0).astype(BF),
                jnp.where(column == block + 2.0, gain[:, ROW:], 0.0).astype(BF),
            ],
            axis=1,
        )
        put = (iota((SLOTS, SLOTS), 0).astype(F32) == across).astype(F32).astype(BF)
        totals_v[...] += jnp.dot(put, gain, preferred_element_type=F32)
        return 0

    lax.fori_loop(0, BATCHES, settle, 0)

    for q in range(4):
        rows = slice((q // 2) * 256, (q // 2) * 256 + 256)
        cols = slice((q % 2) * ROW, (q % 2) * ROW + ROW)
        quarter_v[q] = totals_v[rows, cols].astype(BF)
    for d in range(4):
        v = lax.rem(x + d, 4)
        if d == 0:
            pltpu.make_async_copy(quarter_v.at[v], placed_v.at[x], tot_sem.at[0]).start()
        else:
            pltpu.make_async_remote_copy(
                src_ref=quarter_v.at[v],
                dst_ref=placed_v.at[x],
                send_sem=sent_sem.at[3],
                recv_sem=tot_sem.at[0],
                device_id=(surf, v),
                device_id_type=MESH,
            ).start()

    def collect(g, _):
        span = pl.ds(pl.multiple_of(g * BATCH, BATCH), BATCH)
        wait_for(back_v.at[span], ans_sem.at[g])
        lanes = iota((SEGS, ROW), 1) + g * SLOTS
        slots = slotrep_v[...]
        pick = jnp.concatenate(
            [(slots == lanes + t * ROW).astype(F32).astype(BF) for t in range(SLOTS // ROW)], axis=1
        )
        acc_v[...] += jnp.dot(pick, back_v[span].reshape(SLOTS, ROW), preferred_element_type=F32)
        return 0

    lax.fori_loop(0, BATCHES - 2, collect, 0)

    loads[3].wait()
    wait_for(placed_v, tot_sem.at[0])
    for u in range(4):
        for half in range(2):
            rows = slice(u * QUARTER + half * 256, u * QUARTER + half * 256 + 256)
            volume = volume_v[rows, :]
            both = jnp.concatenate([placed_v[u], volume], axis=1)
            change = jnp.dot(both, wcond_v[half], preferred_element_type=F32)
            mout_v[rows, :] = (volume.astype(F32) + change).astype(BF)
    mold_store = pltpu.make_async_copy(mout_v, mout_hbm, out_sem.at[0])
    mold_store.start()

    lax.fori_loop(BATCHES - 2, BATCHES, collect, 0)
    cout_v[...] = acc_v[...].astype(BF)
    casting_store = pltpu.make_async_copy(cout_v, cout_hbm, out_sem.at[1])
    casting_store.start()
    wait_for(ids_send.at[pl.ds(1, PEERS - 1)], sent_sem.at[0])
    wait_for(send_v.at[pl.ds(1, PEERS - 1)], sent_sem.at[1])
    wait_for(ans_v.at[pl.ds(1, PEERS - 1)], sent_sem.at[2])
    wait_for(quarter_v.at[pl.ds(0, 3)], sent_sem.at[3])
    mold_store.wait()
    casting_store.wait()


def local(casting, owner, face_id, mold_faces, mortar_d, mortar_m, conduct, volume):
    vmem = pl.BlockSpec(memory_space=pltpu.VMEM)
    hbm = pl.BlockSpec(memory_space=pl.ANY)
    slots = (PEERS, PER, ROW)
    return pl.pallas_call(
        kernel,
        out_shape=(
            jax.ShapeDtypeStruct((SEGS, ROW), BF),
            jax.ShapeDtypeStruct((FACES, ROW), BF),
        ),
        in_specs=[vmem] * 5 + [hbm] * 3,
        out_specs=(hbm, hbm),
        scratch_shapes=[
            pltpu.VMEM((SEGS, ROW), BF),
            pltpu.VMEM((1024, 2 * ROW), BF),
            pltpu.VMEM((FACES, ROW), BF),
            pltpu.VMEM(slots, BF),
            pltpu.VMEM(slots, BF),
            pltpu.VMEM(slots, BF),
            pltpu.VMEM(slots, BF),
            pltpu.VMEM((PEERS, ROW), F32),
            pltpu.VMEM((PEERS, ROW), F32),
            pltpu.VMEM((ROW, 2 * ROW), BF),
            pltpu.VMEM((ROW, 2 * ROW), BF),
            pltpu.VMEM((2, 2 * ROW, ROW), BF),
            pltpu.VMEM((ROW, SLOTS), BF),
            pltpu.VMEM((ROW, 2 * ROW), BF),
            pltpu.VMEM((8, ROW), F32),
            pltpu.VMEM((SEGS, ROW), I32),
            pltpu.VMEM((SLOTS, 2 * ROW), F32),
            pltpu.VMEM((4, 256, ROW), BF),
            pltpu.VMEM((4, 256, ROW), BF),
            pltpu.VMEM((SEGS, ROW), F32),
            pltpu.VMEM((SEGS, ROW), BF),
            pltpu.VMEM((FACES, ROW), BF),
            pltpu.SemaphoreType.DMA((4,)),
            pltpu.SemaphoreType.DMA((2,)),
            pltpu.SemaphoreType.DMA((BATCHES,)),
            pltpu.SemaphoreType.DMA((BATCHES,)),
            pltpu.SemaphoreType.DMA((BATCHES,)),
            pltpu.SemaphoreType.DMA((1,)),
            pltpu.SemaphoreType.DMA((4,)),
        ],
        compiler_params=pltpu.CompilerParams(
            collective_id=0, has_side_effects=True, vmem_limit_bytes=40 * 2**20
        ),
        cost_estimate=pl.CostEstimate(
            flops=2 * 4096 * 1024 * 1024, bytes_accessed=2 * 2**20, transcendentals=0
        ),
    )(
        owner.reshape(8, ROW),
        face_id.reshape(8, ROW),
        mortar_d,
        mortar_m,
        conduct,
        casting,
        mold_faces,
        volume,
    )


def solution(mesh):
    rows, flat = P(("surf", "vol"), None), P(("surf", "vol"))
    return jax.shard_map(
        local,
        mesh=mesh,
        in_specs=(rows, rows, flat, rows, P(), P(), P(), rows),
        out_specs=(rows, rows),
        check_vma=False,
    )
```

time: 121 us -> 50 us (0.41)
  waiting for transfers between devices: 41.1 us -> 0 us
  Pallas kernels: 0 us -> 40.8 us
  matrix products: 21.3 us -> 0 us
  starting transfers between devices: 21.3 us -> 0 us
  local copies, waits for them, and re-layouts: 24.7 us -> 8.09 us
  blocking collectives: 8.62 us -> 0 us
  other arithmetic: 1.76 us -> 0 us
    all_to_all x3 -> x0, waiting for transfers between devices: 41.1 us -> none  [the longest x1 18.3 us: local(): lax.all_to_all(answers.reshape(devices, capacity, row_width), ('surf', 'v...]
    pallas_call x0 -> x1, Pallas kernels: none -> 40.8 us  [local(): pl.pallas_call(kernel, out_shape=(jax.ShapeDtypeStruct((SEGS, ROW), BF),...]
    dot_general x33 -> x0, matrix products: 21.3 us -> none  [the longest x8 8.6 us: settle(): jnp.dot(selector, mold_faces, preferred_element_type=jnp.float32)]
    all_to_all x3 -> x0, starting transfers between devices: 21.3 us -> none  [the longest x1 11.5 us: local(): lax.all_to_all(send_ids.reshape(devices, capacity), ('surf', 'vol'), spli...]
    scatter x2 -> x0, local copies, waits for them, and re-layouts: 9.18 us -> none  [the longest x1 4.69 us: local(): jnp.zeros((slots, row_width), jnp.bfloat16).at[slot_index].set(casting)]
    all_to_all x1 -> x0, blocking collectives: 8.62 us -> none  [local(): lax.all_to_all(face_totals.reshape(vol_count, quarter * node_count // row...]
    unnamed x14 -> x18, local copies, waits for them, and re-layouts: 0.73 us -> 8.09 us
    dynamic_update_slice x16 -> x0, local copies, waits for them, and re-layouts: 6.25 us -> none  [local(): lax.scan(settle, jnp.zeros((face_rows, node_count), jnp.float32), (flat_r...]
  transfers between devices with their start and end apart: 3 -> 0, of which waited for: 3 -> 0; matrix products, arithmetic and copies ran while one was open for 6% -> 0% of each run, Pallas kernels for 0% -> 0%
where the time goes in v1:
time: 50 us; the launch traced here: 49.5 us
  Pallas kernels  40.8 us (82%)
  local copies, waits for them, and re-layouts  8.09 us (16%)
  between operations  0.66 us (1%)
    pallas_call x1, Pallas kernels, local(): pl.pallas_call(kernel, out_shape=(jax.ShapeDtypeStruct((SEGS, ROW), BF),...  40.8 us
    unnamed x18, local copies, waits for them, and re-layouts  8.09 us

profile of v1, /device:TPU:1, one launch (start us, length us, event | category | flops | bytes accessed | tf_op | source)
XLA Modules:
  0.0 49.5 jit_solution(17020134431262830234)
XLA Ops:
  0.6 0.0 copy-start
  0.6 1.0 %copy-done = bf16[2048,128]{1,0:T(8,128)(2,1)S(1)} copy-done((bf16[2048,128]{1,0:T(8,128)(2,1)S(1)}, bf16[2048,128]{1,0:T(8,128)(2,1)}, u32[]{:S(2)}) %copy-start) | copy-done | bytes 524312
  1.7 0.0 copy-start.1
  1.7 1.0 %copy-done.1 = bf16[2048,128]{1,0:T(8,128)(2,1)S(1)} copy-done((bf16[2048,128]{1,0:T(8,128)(2,1)S(1)}, bf16[2048,128]{1,0:T(8,128)(2,1)}, u32[]{:S(2)}) %copy-start.1) | copy-done | bytes 524312
  2.7 0.0 copy-start.2
  2.7 0.9 %copy-done.2 = bf16[1024,128]{1,0:T(8,128)(2,1)S(1)} copy-done((bf16[1024,128]{1,0:T(8,128)(2,1)S(1)}, bf16[1024,128]{1,0:T(8,128)(2,1)}, u32[]{:S(2)}) %copy-start.2) | copy-done | bytes 262168
  3.7 0.0 copy-start.3
  3.7 0.8 %copy-done.3 = bf16[128,128]{1,0:T(8,128)(2,1)S(1)} copy-done((bf16[128,128]{1,0:T(8,128)(2,1)S(1)}, bf16[128,128]{1,0:T(8,128)(2,1)}, u32[]{:S(2)}) %copy-start.3) | copy-done | bytes 32792
  4.4 0.0 copy-start.4
  4.4 0.7 %copy-done.4 = bf16[64,64]{1,0:T(8,128)(2,1)S(1)} copy-done((bf16[64,64]{1,0:T(8,128)(2,1)S(1)}, bf16[64,64]{1,0:T(8,128)(2,1)}, u32[]{:S(2)}) %copy-start.4) | copy-done | bytes 8216
  5.1 0.0 copy-start.5
  5.1 0.7 %copy-done.5 = bf16[64,64]{1,0:T(8,128)(2,1)S(1)} copy-done((bf16[64,64]{1,0:T(8,128)(2,1)S(1)}, bf16[64,64]{1,0:T(8,128)(2,1)}, u32[]{:S(2)}) %copy-start.5) | copy-done | bytes 8216
  5.9 0.0 copy-start.6
  5.9 0.7 %copy-done.6 = s32[1024,1]{0,1:T(1,128)S(1)} copy-done((s32[1024,1]{0,1:T(1,128)S(1)}, s32[1024,1]{0,1:T(1,128)}, u32[]{:S(2)}) %copy-start.6) | copy-done | bytes 4120
  6.5 0.0 copy-start.7
  6.6 0.7 %copy-done.7 = s32[1024]{0:T(1024)S(1)} copy-done((s32[1024]{0:T(1024)S(1)}, s32[1024]{0:T(1024)}, u32[]{:S(2)}) %copy-start.7) | copy-done | bytes 4120
  7.2 40.8 %shard_map.95 = (bf16[1024,128]{1,0:T(8,128)(2,1)S(1)}, bf16[2048,128]{1,0:T(8,128)(2,1)S(1)}) custom-call(s32[8,128]{1,0:T(8,128)S(1)} %bitcast.2, s32[8,128]{1,0:T(8,128)S(1)} %bitcast.3, bf16[64,64]{1,0:T(8,128)(2,1)S(1)} %copy-done.4, bf16[64,64]{1,0:T(8,128)(2,1)S(1)} %copy-done.5, bf16[128,128]{1,0:T(8,128)(2,1)S(1)} %copy-done.3, ...), custom_call_target="tpu_custom_call" | custom-call | flops 8589934592 | bytes 2097152 | tf_op jit(solution)/shard_map/pallas_call | solution.py:334
  48.0 0.7 %copy.12 = bf16[1024,128]{1,0:T(8,128)(2,1)} copy(bf16[1024,128]{1,0:T(8,128)(2,1)S(1)} %get-tuple-element.4) | data formatting | bytes 524288
  48.7 0.8 %copy.13 = bf16[2048,128]{1,0:T(8,128)(2,1)} copy(bf16[2048,128]{1,0:T(8,128)(2,1)S(1)} %get-tuple-element.5) | data formatting | bytes 1048576
Async XLA Ops:
  0.6 1.0 %copy-start = (bf16[2048,128]{1,0:T(8,128)(2,1)S(1)}, bf16[2048,128]{1,0:T(8,128)(2,1)}, u32[]{:S(2)}) copy-start(bf16[2048,128]{1,0:T(8,128)(2,1)} %mold_hbm.1) | copy-start | bytes 1572868
  1.7 1.0 %copy-start.1 = (bf16[2048,128]{1,0:T(8,128)(2,1)S(1)}, bf16[2048,128]{1,0:T(8,128)(2,1)}, u32[]{:S(2)}) copy-start(bf16[2048,128]{1,0:T(8,128)(2,1)} %volume_hbm.1) | copy-start | bytes 1572868
  2.7 0.9 %copy-start.2 = (bf16[1024,128]{1,0:T(8,128)(2,1)S(1)}, bf16[1024,128]{1,0:T(8,128)(2,1)}, u32[]{:S(2)}) copy-start(bf16[1024,128]{1,0:T(8,128)(2,1)} %casting_hbm.1) | copy-start | bytes 786436
  3.7 0.8 %copy-start.3 = (bf16[128,128]{1,0:T(8,128)(2,1)S(1)}, bf16[128,128]{1,0:T(8,128)(2,1)}, u32[]{:S(2)}) copy-start(bf16[128,128]{1,0:T(8,128)(2,1)} %conduct_ref.1) | copy-start | bytes 98308
  4.4 0.7 %copy-start.4 = (bf16[64,64]{1,0:T(8,128)(2,1)S(1)}, bf16[64,64]{1,0:T(8,128)(2,1)}, u32[]{:S(2)}) copy-start(bf16[64,64]{1,0:T(8,128)(2,1)} %d_ref.1) | copy-start | bytes 24580
  5.1 0.7 %copy-start.5 = (bf16[64,64]{1,0:T(8,128)(2,1)S(1)}, bf16[64,64]{1,0:T(8,128)(2,1)}, u32[]{:S(2)}) copy-start(bf16[64,64]{1,0:T(8,128)(2,1)} %m_ref.1) | copy-start | bytes 24580
  5.9 0.7 %copy-start.6 = (s32[1024,1]{0,1:T(1,128)S(1)}, s32[1024,1]{0,1:T(1,128)}, u32[]{:S(2)}) copy-start(s32[1024,1]{0,1:T(1,128)} %param.9) | copy-start | bytes 12292
  6.5 0.7 %copy-start.7 = (s32[1024]{0:T(1024)S(1)}, s32[1024]{0:T(1024)}, u32[]{:S(2)}) copy-start(s32[1024]{0:T(1024)} %param.10) | copy-start | bytes 12292

commit v2 on v1

--- a/solution.py
+++ b/solution.py
@@ -29,16 +29,21 @@
 
 
 def kernel(
+    owner_hbm,
+    face_hbm,
+    d_hbm,
+    m_hbm,
+    conduct_hbm,
+    casting_hbm,
+    mold_hbm,
+    volume_hbm,
+    cout_hbm,
+    mout_hbm,
     owner_ref,
     face_ref,
     d_ref,
     m_ref,
     conduct_ref,
-    casting_hbm,
-    mold_hbm,
-    volume_hbm,
-    cout_hbm,
-    mout_hbm,
     casting_v,
     mold_v,
     volume_v,
@@ -90,13 +95,25 @@
             else:
                 act(g, i)
 
+    small = [
+        pltpu.make_async_copy(source, place, load_sem.at[4 + n])
+        for n, (source, place) in enumerate(
+            [
+                (owner_hbm, owner_ref),
+                (face_hbm, face_ref),
+                (d_hbm, d_ref),
+                (m_hbm, m_ref),
+                (conduct_hbm, conduct_ref),
+            ]
+        )
+    ]
     loads = [
         pltpu.make_async_copy(casting_hbm, casting_v, load_sem.at[0]),
         pltpu.make_async_copy(mold_hbm.at[pl.ds(0, 1024)], mold_v.at[:, pl.ds(0, ROW)], load_sem.at[1]),
         pltpu.make_async_copy(mold_hbm.at[pl.ds(1024, 1024)], mold_v.at[:, pl.ds(ROW, ROW)], load_sem.at[2]),
         pltpu.make_async_copy(volume_hbm, volume_v, load_sem.at[3]),
     ]
-    for load in loads:
+    for load in small + loads:
         load.start()
 
     barrier = pltpu.get_barrier_semaphore()
@@ -110,6 +127,7 @@
 
     lax.fori_loop(0, BATCHES, greet, 0)
 
+    small[0].wait()
     owner = owner_ref[...]
     dx = (owner & 3) - x & 3
     dc = (owner >> 2 & 1) - c & 1
@@ -129,6 +147,7 @@
     slot8 = (order * PER).astype(F32) + row8_v[...]
     row8_v[...] = slot8
     slot_t = slot8.T
+    small[1].wait()
     face_t = face_ref[...].astype(F32).T
     table = jnp.zeros((PEERS, ROW), F32)
     for b in range(8):
@@ -140,6 +159,8 @@
         table = table + jnp.dot(hits[b], part.astype(F32).astype(BF), preferred_element_type=F32)
     ids_send[...] = table
 
+    for load in small[2:]:
+        load.wait()
     wgap_v[...] = jnp.zeros_like(wgap_v)
     wgap_v[NODES:, 0:NODES] = d_ref[...]
     wgap_v[NODES:, ROW : ROW + NODES] = -m_ref[...]
@@ -328,8 +349,7 @@
 
 
 def local(casting, owner, face_id, mold_faces, mortar_d, mortar_m, conduct, volume):
-    vmem = pl.BlockSpec(memory_space=pltpu.VMEM)
-    hbm = pl.BlockSpec(memory_space=pl.ANY)
+    hbm = pl.BlockSpec(memory_space=pltpu.HBM)
     slots = (PEERS, PER, ROW)
     return pl.pallas_call(
         kernel,
@@ -337,9 +357,14 @@
             jax.ShapeDtypeStruct((SEGS, ROW), BF),
             jax.ShapeDtypeStruct((FACES, ROW), BF),
         ),
-        in_specs=[vmem] * 5 + [hbm] * 3,
+        in_specs=[hbm] * 8,
         out_specs=(hbm, hbm),
         scratch_shapes=[
+            pltpu.VMEM((8, ROW), I32),
+            pltpu.VMEM((8, ROW), I32),
+            pltpu.VMEM((NODES, NODES), BF),
+            pltpu.VMEM((NODES, NODES), BF),
+            pltpu.VMEM((ROW, ROW), BF),
             pltpu.VMEM((SEGS, ROW), BF),
             pltpu.VMEM((1024, 2 * ROW), BF),
             pltpu.VMEM((FACES, ROW), BF),
@@ -362,7 +387,7 @@
             pltpu.VMEM((SEGS, ROW), F32),
             pltpu.VMEM((SEGS, ROW), BF),
             pltpu.VMEM((FACES, ROW), BF),
-            pltpu.SemaphoreType.DMA((4,)),
+            pltpu.SemaphoreType.DMA((9,)),
             pltpu.SemaphoreType.DMA((2,)),
             pltpu.SemaphoreType.DMA((BATCHES,)),
             pltpu.SemaphoreType.DMA((BATCHES,)),
@@ -371,7 +396,7 @@
             pltpu.SemaphoreType.DMA((4,)),
         ],
         compiler_params=pltpu.CompilerParams(
-            collective_id=0, has_side_effects=True, vmem_limit_bytes=40 * 2**20
+            collective_id=0, has_side_effects=True, vmem_limit_bytes=60 * 2**20
         ),
         cost_estimate=pl.CostEstimate(
             flops=2 * 4096 * 1024 * 1024, bytes_accessed=2 * 2**20, transcendentals=0

time: 50 us -> 44.6 us (0.89)
  local copies, waits for them, and re-layouts: 8.09 us -> 2.52 us
  Pallas kernels: 40.8 us -> 41.3 us
    unnamed x18 -> x4, local copies, waits for them, and re-layouts: 8.09 us -> 2.52 us
    pallas_call x1, Pallas kernels: 40.8 us -> 41.3 us  [local(): pl.pallas_call(kernel, out_shape=(jax.ShapeDtypeStruct((SEGS, ROW), BF),...]
where the time goes in v2:
time: 44.6 us; the launch traced here: 44.5 us
  Pallas kernels  41.3 us (93%)
  local copies, waits for them, and re-layouts  2.52 us (6%)
  between operations  0.65 us (1%)
    pallas_call x1, Pallas kernels, local(): pl.pallas_call(kernel, out_shape=(jax.ShapeDtypeStruct((SEGS, ROW), BF),...  41.3 us
    unnamed x4, local copies, waits for them, and re-layouts  2.52 us

profile of v2, /device:TPU:1, one launch (start us, length us, event | category | flops | bytes accessed | tf_op | source)
XLA Modules:
  0.0 44.5 jit_solution(16490037935490451360)
XLA Ops:
  0.6 41.3 %shard_map.95 = (bf16[1024,128]{1,0:T(8,128)(2,1)}, bf16[2048,128]{1,0:T(8,128)(2,1)}) custom-call(s32[8,128]{1,0:T(8,128)} %bitcast.2, s32[8,128]{1,0:T(8,128)} %bitcast.3, bf16[64,64]{1,0:T(8,128)(2,1)} %d_hbm.1, bf16[64,64]{1,0:T(8,128)(2,1)} %m_hbm.1, bf16[128,128]{1,0:T(8,128)(2,1)} %conduct_hbm.1, bf16[1024,128]{1,0:T(8,128)(2,1)} %casting_hbm.1, ...), custom_call_target="tpu_custom_call" | custom-call | flops 8589934592 | bytes 2097152 | tf_op jit(solution)/shard_map/pallas_call | solution.py:354
  42.0 0.0 copy-start
  42.0 1.7 %copy.12 = bf16[1024,128]{1,0:T(8,128)(2,1)} copy(bf16[1024,128]{1,0:T(8,128)(2,1)} %get-tuple-element.4) | data formatting | bytes 524288
  43.7 0.0 copy-done
  43.7 0.8 %copy.13 = bf16[2048,128]{1,0:T(8,128)(2,1)} copy(bf16[2048,128]{1,0:T(8,128)(2,1)S(1)} %copy-done) | data formatting | bytes 1048576
Async XLA Ops:
  42.0 1.7 %copy-start = (bf16[2048,128]{1,0:T(8,128)(2,1)S(1)}, bf16[2048,128]{1,0:T(8,128)(2,1)}, u32[]{:S(2)}) copy-start(bf16[2048,128]{1,0:T(8,128)(2,1)} %get-tuple-element.5) | copy-start | bytes 1572868

commit v3 on v2

--- a/solution.py
+++ b/solution.py
@@ -37,8 +37,8 @@
     casting_hbm,
     mold_hbm,
     volume_hbm,
-    cout_hbm,
-    mout_hbm,
+    cout_v,
+    mout_v,
     owner_ref,
     face_ref,
     d_ref,
@@ -64,10 +64,7 @@
     quarter_v,
     placed_v,
     acc_v,
-    cout_v,
-    mout_v,
     load_sem,
-    out_sem,
     row_sem,
     id_sem,
     ans_sem,
@@ -78,22 +75,32 @@
     x = lax.axis_index("vol")
     z, y, c = surf // 8, lax.rem(surf // 2, 4), lax.rem(surf, 2)
 
-    def peer(g, i, sign):
-        dz, dy = i // 4, i % 4
-        pz = lax.rem(z + 4 + sign * dz, 4)
-        py = lax.rem(y + 4 + sign * dy, 4)
-        px = lax.rem(x + 16 + sign * (g // 2 + dz + dy), 4)
-        pc = lax.rem(c + lax.rem(g, 2) + dz, 2)
-        return (pz * 8 + py * 2 + pc, px)
-
-    def each_peer(g, act, own):
+    along_z = {n: [lax.rem(z + 4 + n * d, 4) * 8 for d in range(4)] for n in (1, -1)}
+    along_y = {n: [lax.rem(y + 4 + n * d, 4) * 2 for d in range(4)] for n in (1, -1)}
+
+    def peers(g, sign):
+        along_x = [lax.rem(x + 16 + sign * (g // 2 + d), 4) for d in range(4)]
+        core = [lax.rem(c + g + d, 2) for d in range(2)]
+        found = []
         for i in range(BATCH):
-            if i == 0:
-                pl.when(g > 0)(functools.partial(act, g, i))
+            dz, dy = i // 4, i % 4
+            found.append((along_z[sign][dz] + along_y[sign][dy] + core[dz % 2], along_x[(dz + dy) % 4]))
+        return found
+
+    def each_peer(g, sign, act, own):
+        found = peers(g, sign)
+        for i in range(BATCH):
+            if i > 0:
+                act(g * BATCH + i, found[i])
+            elif isinstance(g, int):
+                if g > 0:
+                    act(g * BATCH, found[0])
+                elif own is not None:
+                    own()
+            else:
+                pl.when(g > 0)(functools.partial(act, g * BATCH, found[0]))
                 if own is not None:
                     pl.when(g == 0)(own)
-            else:
-                act(g, i)
 
     small = [
         pltpu.make_async_copy(source, place, load_sem.at[4 + n])
@@ -118,14 +125,11 @@
 
     barrier = pltpu.get_barrier_semaphore()
 
-    def greet(g, _):
-        def one(g, i):
-            pl.semaphore_signal(barrier, inc=1, device_id=peer(g, i, 1), device_id_type=MESH)
-
-        each_peer(g, one, None)
-        return 0
-
-    lax.fori_loop(0, BATCHES, greet, 0)
+    def greet(_, to):
+        pl.semaphore_signal(barrier, inc=1, device_id=to, device_id_type=MESH)
+
+    for g in range(BATCHES):
+        each_peer(g, 1, greet, None)
 
     small[0].wait()
     owner = owner_ref[...]
@@ -159,6 +163,55 @@
         table = table + jnp.dot(hits[b], part.astype(F32).astype(BF), preferred_element_type=F32)
     ids_send[...] = table
 
+    loads[0].wait()
+
+    def pack(g, _):
+        want = iota((SLOTS, ROW), 0) + g * SLOTS
+        want = want.astype(F32)
+        pick = jnp.concatenate(
+            [(want == row8_v[b : b + 1, :]).astype(F32).astype(BF) for b in range(8)], axis=1
+        )
+        rows = jnp.dot(pick, casting_v[...], preferred_element_type=F32).astype(BF)
+        send_v[pl.ds(g * BATCH, BATCH)] = rows.reshape(BATCH, PER, ROW)
+        return 0
+
+    pack(0, 0)
+    pack(1, 0)
+    pl.semaphore_wait(barrier, PEERS - 1)
+
+    def send(g, _):
+        def one(j, to):
+            pltpu.make_async_remote_copy(
+                src_ref=ids_send.at[pl.ds(j, 1)],
+                dst_ref=ids_recv.at[pl.ds(j, 1)],
+                send_sem=sent_sem.at[0],
+                recv_sem=id_sem.at[g],
+                device_id=to,
+                device_id_type=MESH,
+            ).start()
+            pltpu.make_async_remote_copy(
+                src_ref=send_v.at[j],
+                dst_ref=recv_v.at[j],
+                send_sem=sent_sem.at[1],
+                recv_sem=row_sem.at[g],
+                device_id=to,
+                device_id_type=MESH,
+            ).start()
+
+        def own():
+            pltpu.make_async_copy(ids_send.at[pl.ds(0, 1)], ids_recv.at[pl.ds(0, 1)], id_sem.at[0]).start()
+            pltpu.make_async_copy(send_v.at[0], recv_v.at[0], row_sem.at[0]).start()
+
+        each_peer(g, 1, one, own)
+
+        @pl.when(g < BATCHES - 2)
+        def _():
+            pack(g + 2, 0)
+
+        return 0
+
+    lax.fori_loop(0, BATCHES, send, 0)
+
     for load in small[2:]:
         load.wait()
     wgap_v[...] = jnp.zeros_like(wgap_v)
@@ -186,50 +239,6 @@
     totals_v[...] = jnp.zeros_like(totals_v)
     acc_v[...] = jnp.zeros_like(acc_v)
 
-    loads[0].wait()
-
-    def pack(g, _):
-        want = iota((SLOTS, ROW), 0) + g * SLOTS
-        want = want.astype(F32)
-        pick = jnp.concatenate(
-            [(want == row8_v[b : b + 1, :]).astype(F32).astype(BF) for b in range(8)], axis=1
-        )
-        rows = jnp.dot(pick, casting_v[...], preferred_element_type=F32).astype(BF)
-        send_v[pl.ds(g * BATCH, BATCH)] = rows.reshape(BATCH, PER, ROW)
-        return 0
-
-    lax.fori_loop(0, BATCHES, pack, 0)
-    pl.semaphore_wait(barrier, PEERS - 1)
-
-    def send(g, _):
-        def one(g, i):
-            j = g * BATCH + i
-            to = peer(g, i, 1)
-            pltpu.make_async_remote_copy(
-                src_ref=ids_send.at[pl.ds(j, 1)],
-                dst_ref=ids_recv.at[pl.ds(j, 1)],
-                send_sem=sent_sem.at[0],
-                recv_sem=id_sem.at[g],
-                device_id=to,
-                device_id_type=MESH,
-            ).start()
-            pltpu.make_async_remote_copy(
-                src_ref=send_v.at[j],
-                dst_ref=recv_v.at[j],
-                send_sem=sent_sem.at[1],
-                recv_sem=row_sem.at[g],
-                device_id=to,
-                device_id_type=MESH,
-            ).start()
-
-        def own():
-            pltpu.make_async_copy(ids_send.at[pl.ds(0, 1)], ids_recv.at[pl.ds(0, 1)], id_sem.at[0]).start()
-            pltpu.make_async_copy(send_v.at[0], recv_v.at[0], row_sem.at[0]).start()
-
-        each_peer(g, one, own)
-        return 0
-
-    lax.fori_loop(0, BATCHES, send, 0)
     loads[1].wait()
     loads[2].wait()
 
@@ -262,21 +271,20 @@
         answer = (back + gap).astype(BF)
         ans_v[span] = answer.reshape(BATCH, PER, ROW)
 
-        def one(g, i):
-            j = g * BATCH + i
+        def one(j, to):
             pltpu.make_async_remote_copy(
                 src_ref=ans_v.at[j],
                 dst_ref=back_v.at[j],
                 send_sem=sent_sem.at[2],
                 recv_sem=ans_sem.at[g],
-                device_id=peer(g, i, -1),
+                device_id=to,
                 device_id_type=MESH,
             ).start()
 
         def own():
             pltpu.make_async_copy(ans_v.at[0], back_v.at[0], ans_sem.at[0]).start()
 
-        each_peer(g, one, own)
+        each_peer(g, -1, one, own)
         gain = jnp.dot(flux, mfour_v[...], preferred_element_type=F32)
         column = jnp.where(upper, high - 4.0, high)
         block = (iota((SLOTS, ROW), 1) >> 6).astype(F32)
@@ -333,23 +341,18 @@
             both = jnp.concatenate([placed_v[u], volume], axis=1)
             change = jnp.dot(both, wcond_v[half], preferred_element_type=F32)
             mout_v[rows, :] = (volume.astype(F32) + change).astype(BF)
-    mold_store = pltpu.make_async_copy(mout_v, mout_hbm, out_sem.at[0])
-    mold_store.start()
 
     lax.fori_loop(BATCHES - 2, BATCHES, collect, 0)
     cout_v[...] = acc_v[...].astype(BF)
-    casting_store = pltpu.make_async_copy(cout_v, cout_hbm, out_sem.at[1])
-    casting_store.start()
     wait_for(ids_send.at[pl.ds(1, PEERS - 1)], sent_sem.at[0])
     wait_for(send_v.at[pl.ds(1, PEERS - 1)], sent_sem.at[1])
     wait_for(ans_v.at[pl.ds(1, PEERS - 1)], sent_sem.at[2])
     wait_for(quarter_v.at[pl.ds(0, 3)], sent_sem.at[3])
-    mold_store.wait()
-    casting_store.wait()
 
 
 def local(casting, owner, face_id, mold_faces, mortar_d, mortar_m, conduct, volume):
     hbm = pl.BlockSpec(memory_space=pltpu.HBM)
+    vmem = pl.BlockSpec(memory_space=pltpu.VMEM)
     slots = (PEERS, PER, ROW)
     return pl.pallas_call(
         kernel,
@@ -358,7 +361,7 @@
             jax.ShapeDtypeStruct((FACES, ROW), BF),
         ),
         in_specs=[hbm] * 8,
-        out_specs=(hbm, hbm),
+        out_specs=(vmem, vmem),
         scratch_shapes=[
             pltpu.VMEM((8, ROW), I32),
             pltpu.VMEM((8, ROW), I32),
@@ -385,10 +388,7 @@
             pltpu.VMEM((4, 256, ROW), BF),
             pltpu.VMEM((4, 256, ROW), BF),
             pltpu.VMEM((SEGS, ROW), F32),
-            pltpu.VMEM((SEGS, ROW), BF),
-            pltpu.VMEM((FACES, ROW), BF),
             pltpu.SemaphoreType.DMA((9,)),
-            pltpu.SemaphoreType.DMA((2,)),
             pltpu.SemaphoreType.DMA((BATCHES,)),
             pltpu.SemaphoreType.DMA((BATCHES,)),
             pltpu.SemaphoreType.DMA((BATCHES,)),
@@ -396,20 +396,25 @@
             pltpu.SemaphoreType.DMA((4,)),
         ],
         compiler_params=pltpu.CompilerParams(
-            collective_id=0, has_side_effects=True, vmem_limit_bytes=60 * 2**20
+            collective_id=0, has_side_effects=True, vmem_limit_bytes=40 * 2**20
         ),
         cost_estimate=pl.CostEstimate(
             flops=2 * 4096 * 1024 * 1024, bytes_accessed=2 * 2**20, transcendentals=0
         ),
     )(
-        owner.reshape(8, ROW),
-        face_id.reshape(8, ROW),
-        mortar_d,
-        mortar_m,
-        conduct,
-        casting,
-        mold_faces,
-        volume,
+        *(
+            pltpu.with_memory_space_constraint(a, pltpu.HBM)
+            for a in (
+                owner.reshape(8, ROW),
+                face_id.reshape(8, ROW),
+                mortar_d,
+                mortar_m,
+                conduct,
+                casting,
+                mold_faces,
+                volume,
+            )
+        )
     )
 
 

time: 44.6 us -> 43.2 us (0.969)
  local copies, waits for them, and re-layouts: 2.52 us -> 1.5 us
    unnamed x4 -> x2, local copies, waits for them, and re-layouts: 2.52 us -> 1.5 us
where the time goes in v3:
time: 43.2 us; the launch traced here: 43.1 us
  Pallas kernels  40.9 us (95%)
  local copies, waits for them, and re-layouts  1.5 us (3%)
  between operations  0.64 us (1%)
    pallas_call x1, Pallas kernels, local(): pl.pallas_call(kernel, out_shape=(jax.ShapeDtypeStruct((SEGS, ROW), BF),...  40.9 us
    unnamed x2, local copies, waits for them, and re-layouts  1.5 us

profile of v3, /device:TPU:1, one launch (start us, length us, event | category | flops | bytes accessed | tf_op | source)
XLA Modules:
  0.0 43.1 jit_solution(17754902340517308403)
XLA Ops:
  0.6 40.9 %shard_map.95 = (bf16[1024,128]{1,0:T(8,128)(2,1)S(1)}, bf16[2048,128]{1,0:T(8,128)(2,1)S(1)}) custom-call(s32[8,128]{1,0:T(8,128)} %bitcast.2, s32[8,128]{1,0:T(8,128)} %bitcast.3, bf16[64,64]{1,0:T(8,128)(2,1)} %d_hbm.1, bf16[64,64]{1,0:T(8,128)(2,1)} %m_hbm.1, bf16[128,128]{1,0:T(8,128)(2,1)} %conduct_hbm.1, bf16[1024,128]{1,0:T(8,128)(2,1)} %casting_hbm.1, ...), custom_call_target="tpu_custom_call" | custom-call | flops 8589934592 | bytes 2097152 | tf_op jit(solution)/shard_map/pallas_call | solution.py:357
  41.6 0.7 %copy.12 = bf16[1024,128]{1,0:T(8,128)(2,1)} copy(bf16[1024,128]{1,0:T(8,128)(2,1)S(1)} %get-tuple-element.4) | data formatting | bytes 524288
  42.3 0.8 %copy.13 = bf16[2048,128]{1,0:T(8,128)(2,1)} copy(bf16[2048,128]{1,0:T(8,128)(2,1)S(1)} %get-tuple-element.5) | data formatting | bytes 1048576

commit v4 on v3

--- a/solution.py
+++ b/solution.py
@@ -1,7 +1,9 @@
 import functools
+import itertools
 
 import jax
 import jax.numpy as jnp
+import numpy as np
 from jax import lax
 from jax.experimental import pallas as pl
 from jax.experimental.pallas import tpu as pltpu
@@ -24,6 +26,31 @@
 QUARTER = FACES // 4
 
 
+def hops(offset):
+    dz, dy, _, dx = offset
+    return sum(min(d, 4 - d) for d in (dz, dy, dx))
+
+
+def in_order():
+    offsets = list(itertools.product(range(4), range(4), range(2), range(4)))
+    rest = offsets[1:]
+    def key(o):
+        dz, dy, dc, dx = o
+        return ((dx - dz - dy & 3) * 2 + (dc - dz & 1)) * 16 + dz * 4 + dy
+    rest.sort(key=key)
+    return offsets[:1] + rest
+
+
+ORDER = in_order()
+PLACE = np.zeros((8, 128), np.float32)
+for at, (oz, oy, oc, ox) in enumerate(ORDER):
+    PLACE[:, ((oz * 4 + oy) * 2 + oc) * 4 + ox] = at
+PACKED = [
+    [sum(ORDER[g * BATCH + i][n] << 2 * g for g in range(BATCHES)) for i in range(BATCH)]
+    for n in range(4)
+]
+
+
 def iota(shape, dim):
     return lax.broadcasted_iota(I32, shape, dim)
 
@@ -31,6 +58,7 @@
 def kernel(
     owner_hbm,
     face_hbm,
+    place_hbm,
     d_hbm,
     m_hbm,
     conduct_hbm,
@@ -41,6 +69,7 @@
     mout_v,
     owner_ref,
     face_ref,
+    place_ref,
     d_ref,
     m_ref,
     conduct_ref,
@@ -75,30 +104,27 @@
     x = lax.axis_index("vol")
     z, y, c = surf // 8, lax.rem(surf // 2, 4), lax.rem(surf, 2)
 
-    along_z = {n: [lax.rem(z + 4 + n * d, 4) * 8 for d in range(4)] for n in (1, -1)}
-    along_y = {n: [lax.rem(y + 4 + n * d, 4) * 2 for d in range(4)] for n in (1, -1)}
-
     def peers(g, sign):
-        along_x = [lax.rem(x + 16 + sign * (g // 2 + d), 4) for d in range(4)]
-        core = [lax.rem(c + g + d, 2) for d in range(2)]
         found = []
         for i in range(BATCH):
-            dz, dy = i // 4, i % 4
-            found.append((along_z[sign][dz] + along_y[sign][dy] + core[dz % 2], along_x[(dz + dy) % 4]))
+            if isinstance(g, int):
+                dz, dy, dc, dx = ORDER[g * BATCH + i]
+            else:
+                dz, dy, dc, dx = (packed[i] >> (2 * g) & 3 for packed in PACKED)
+            pz, py, pc, px = z + sign * dz & 3, y + sign * dy & 3, c + dc & 1, x + sign * dx & 3
+            found.append((((pz * 8 + py * 2 + pc, px)), ((dz * 4 + dy) * 2 + dc) * 4 + dx))
         return found
 
     def each_peer(g, sign, act, own):
         found = peers(g, sign)
         for i in range(BATCH):
             if i > 0:
-                act(g * BATCH + i, found[i])
+                act(g * BATCH + i, *found[i])
             elif isinstance(g, int):
                 if g > 0:
-                    act(g * BATCH, found[0])
-                elif own is not None:
-                    own()
+                    act(g * BATCH, *found[0])
             else:
-                pl.when(g > 0)(functools.partial(act, g * BATCH, found[0]))
+                pl.when(g > 0)(functools.partial(act, g * BATCH, *found[0]))
                 if own is not None:
                     pl.when(g == 0)(own)
 
@@ -108,6 +134,7 @@
             [
                 (owner_hbm, owner_ref),
                 (face_hbm, face_ref),
+                (place_hbm, place_ref),
                 (d_hbm, d_ref),
                 (m_hbm, m_ref),
                 (conduct_hbm, conduct_ref),
@@ -125,11 +152,11 @@
 
     barrier = pltpu.get_barrier_semaphore()
 
-    def greet(_, to):
+    far_first = sorted(range(1, PEERS), key=lambda j: -hops(ORDER[j]))
+    for j in far_first:
+        dz, dy, dc, dx = ORDER[j]
+        to = ((z + dz & 3) * 8 + (y + dy & 3) * 2 + (c + dc & 1), x + dx & 3)
         pl.semaphore_signal(barrier, inc=1, device_id=to, device_id_type=MESH)
-
-    for g in range(BATCHES):
-        each_peer(g, 1, greet, None)
 
     small[0].wait()
     owner = owner_ref[...]
@@ -137,19 +164,21 @@
     dc = (owner >> 2 & 1) - c & 1
     dy = (owner >> 3 & 3) - y & 3
     dz = (owner >> 5 & 3) - z & 3
-    order = (dx - dz - dy & 3) * 32 + (dc - dz & 1) * 16 + dz * 4 + dy
+    offset = ((dz * 4 + dy) * 2 + dc) * 4 + dx
     down, lane = iota((ROW, ROW), 0), iota((ROW, ROW), 1)
     before = jnp.concatenate([(down < lane).astype(F32), jnp.ones((ROW, ROW), F32)], axis=1).astype(BF)
+    small[2].wait()
+    place = place_ref[...].astype(BF)
     hits, sofar = [], jnp.zeros((PEERS, ROW), F32)
     for b in range(8):
-        hit = down == order[b : b + 1, :]
+        hit = down == offset[b : b + 1, :]
         hits.append(hit.astype(F32).astype(BF))
         count = jnp.dot(hits[b], before, preferred_element_type=F32)
         rank = jnp.sum(jnp.where(hit, count[:, :ROW] + sofar, 0.0), axis=0, keepdims=True)
         sofar = sofar + count[:, ROW:]
-        row8_v[b : b + 1, :] = rank
-    slot8 = (order * PER).astype(F32) + row8_v[...]
-    row8_v[...] = slot8
+        order = jnp.dot(place, hits[b], preferred_element_type=F32)[0:1]
+        row8_v[b : b + 1, :] = order * PER + rank
+    slot8 = row8_v[...]
     slot_t = slot8.T
     small[1].wait()
     face_t = face_ref[...].astype(F32).T
@@ -180,9 +209,9 @@
     pl.semaphore_wait(barrier, PEERS - 1)
 
     def send(g, _):
-        def one(j, to):
+        def one(j, to, k):
             pltpu.make_async_remote_copy(
-                src_ref=ids_send.at[pl.ds(j, 1)],
+                src_ref=ids_send.at[pl.ds(k, 1)],
                 dst_ref=ids_recv.at[pl.ds(j, 1)],
                 send_sem=sent_sem.at[0],
                 recv_sem=id_sem.at[g],
@@ -212,7 +241,7 @@
 
     lax.fori_loop(0, BATCHES, send, 0)
 
-    for load in small[2:]:
+    for load in small[3:]:
         load.wait()
     wgap_v[...] = jnp.zeros_like(wgap_v)
     wgap_v[NODES:, 0:NODES] = d_ref[...]
@@ -271,7 +300,7 @@
         answer = (back + gap).astype(BF)
         ans_v[span] = answer.reshape(BATCH, PER, ROW)
 
-        def one(j, to):
+        def one(j, to, k):
             pltpu.make_async_remote_copy(
                 src_ref=ans_v.at[j],
                 dst_ref=back_v.at[j],
@@ -350,21 +379,33 @@
     wait_for(quarter_v.at[pl.ds(0, 3)], sent_sem.at[3])
 
 
+def store(cast_in, mold_in, cast_out, mold_out, sem):
+    copies = [
+        pltpu.make_async_copy(cast_in, cast_out, sem.at[0]),
+        pltpu.make_async_copy(mold_in, mold_out, sem.at[1]),
+    ]
+    for copy in copies:
+        copy.start()
+    for copy in copies:
+        copy.wait()
+
+
 def local(casting, owner, face_id, mold_faces, mortar_d, mortar_m, conduct, volume):
     hbm = pl.BlockSpec(memory_space=pltpu.HBM)
     vmem = pl.BlockSpec(memory_space=pltpu.VMEM)
     slots = (PEERS, PER, ROW)
-    return pl.pallas_call(
+    made = pl.pallas_call(
         kernel,
         out_shape=(
             jax.ShapeDtypeStruct((SEGS, ROW), BF),
             jax.ShapeDtypeStruct((FACES, ROW), BF),
         ),
-        in_specs=[hbm] * 8,
+        in_specs=[hbm] * 9,
         out_specs=(vmem, vmem),
         scratch_shapes=[
             pltpu.VMEM((8, ROW), I32),
             pltpu.VMEM((8, ROW), I32),
+            pltpu.VMEM((8, ROW), F32),
             pltpu.VMEM((NODES, NODES), BF),
             pltpu.VMEM((NODES, NODES), BF),
             pltpu.VMEM((ROW, ROW), BF),
@@ -388,7 +429,7 @@
             pltpu.VMEM((4, 256, ROW), BF),
             pltpu.VMEM((4, 256, ROW), BF),
             pltpu.VMEM((SEGS, ROW), F32),
-            pltpu.SemaphoreType.DMA((9,)),
+            pltpu.SemaphoreType.DMA((10,)),
             pltpu.SemaphoreType.DMA((BATCHES,)),
             pltpu.SemaphoreType.DMA((BATCHES,)),
             pltpu.SemaphoreType.DMA((BATCHES,)),
@@ -407,6 +448,7 @@
             for a in (
                 owner.reshape(8, ROW),
                 face_id.reshape(8, ROW),
+                jnp.asarray(PLACE),
                 mortar_d,
                 mortar_m,
                 conduct,
@@ -416,6 +458,16 @@
             )
         )
     )
+    return pl.pallas_call(
+        store,
+        out_shape=(
+            jax.ShapeDtypeStruct((SEGS, ROW), BF),
+            jax.ShapeDtypeStruct((FACES, ROW), BF),
+        ),
+        in_specs=[vmem] * 2,
+        out_specs=(hbm, hbm),
+        scratch_shapes=[pltpu.SemaphoreType.DMA((2,))],
+    )(*(pltpu.with_memory_space_constraint(a, pltpu.VMEM) for a in made))
 
 
 def solution(mesh):

time: 43.2 us -> 41.4 us (0.958)
  local copies, waits for them, and re-layouts: 1.5 us -> 0 us
    unnamed x2 -> x0, local copies, waits for them, and re-layouts: 1.5 us -> none
    pallas_call x1, Pallas kernels: 40.9 us -> 39.8 us  [local(): pl.pallas_call(kernel, out_shape=(jax.ShapeDtypeStruct((SEGS, ROW), BF),...]
    pallas_call x0 -> x1, Pallas kernels: none -> 0.9 us  [local(): pl.pallas_call(store, out_shape=(jax.ShapeDtypeStruct((SEGS, ROW), BF), j...]
where the time goes in v4:
time: 41.4 us; the launch traced here: 41.3 us
  Pallas kernels  40.7 us (98%)
  between operations  0.64 us (2%)
    pallas_call x1, Pallas kernels, local(): pl.pallas_call(kernel, out_shape=(jax.ShapeDtypeStruct((SEGS, ROW), BF),...  39.8 us
    pallas_call x1, Pallas kernels, local(): pl.pallas_call(store, out_shape=(jax.ShapeDtypeStruct((SEGS, ROW), BF), j...  0.9 us

profile of v4, /device:TPU:1, one launch (start us, length us, event | category | flops | bytes accessed | tf_op | source)
XLA Modules:
  0.0 41.3 jit_solution(12397435681409261427)
XLA Ops:
  0.6 39.8 %shard_map.104 = (bf16[1024,128]{1,0:T(8,128)(2,1)S(1)}, bf16[2048,128]{1,0:T(8,128)(2,1)S(1)}) custom-call(s32[8,128]{1,0:T(8,128)} %bitcast.2, s32[8,128]{1,0:T(8,128)} %bitcast.3, f32[8,128]{1,0:T(8,128)} %constant.2.clone.place_hbm, bf16[64,64]{1,0:T(8,128)(2,1)} %d_hbm.1, bf16[64,64]{1,0:T(8,128)(2,1)} %m_hbm.1, bf16[128,128]{1,0:T(8,128)(2,1)} %conduct_hbm.1, ...), custom_call_target="tpu_custom_call" | custom-call | flops 8589934592 | bytes 2097152 | tf_op jit(solution)/shard_map/pallas_call | solution.py:397
  40.4 0.9 %shard_map.105 = (bf16[1024,128]{1,0:T(8,128)(2,1)}, bf16[2048,128]{1,0:T(8,128)(2,1)}) custom-call(bf16[1024,128]{1,0:T(8,128)(2,1)S(1)} %get-tuple-element.4.cast_in, bf16[2048,128]{1,0:T(8,128)(2,1)S(1)} %get-tuple-element.5.mold_in), custom_call_target="tpu_custom_call" | custom-call | tf_op jit(solution)/shard_map/pallas_call | solution.py:461

commit v5 on v4

--- a/solution.py
+++ b/solution.py
@@ -36,7 +36,7 @@
     rest = offsets[1:]
     def key(o):
         dz, dy, dc, dx = o
-        return ((dx - dz - dy & 3) * 2 + (dc - dz & 1)) * 16 + dz * 4 + dy
+        return ((dc - dz & 1) * 4 + (dx - dz - dy & 3)) * 16 + dz * 4 + dy
     rest.sort(key=key)
     return offsets[:1] + rest
 
@@ -361,6 +361,8 @@
 
     lax.fori_loop(0, BATCHES - 2, collect, 0)
 
+    lax.fori_loop(BATCHES - 2, BATCHES, collect, 0)
+    cout_v[...] = acc_v[...].astype(BF)
     loads[3].wait()
     wait_for(placed_v, tot_sem.at[0])
     for u in range(4):
@@ -371,8 +373,6 @@
             change = jnp.dot(both, wcond_v[half], preferred_element_type=F32)
             mout_v[rows, :] = (volume.astype(F32) + change).astype(BF)
 
-    lax.fori_loop(BATCHES - 2, BATCHES, collect, 0)
-    cout_v[...] = acc_v[...].astype(BF)
     wait_for(ids_send.at[pl.ds(1, PEERS - 1)], sent_sem.at[0])
     wait_for(send_v.at[pl.ds(1, PEERS - 1)], sent_sem.at[1])
     wait_for(ans_v.at[pl.ds(1, PEERS - 1)], sent_sem.at[2])

time: 41.4 us -> 40.4 us (0.976)
  Pallas kernels: 40.7 us -> 39.6 us
    pallas_call x1, Pallas kernels: 39.8 us -> 38.7 us  [local(): pl.pallas_call(kernel, out_shape=(jax.ShapeDtypeStruct((SEGS, ROW), BF),...]
where the time goes in v5:
time: 40.4 us; the launch traced here: 40.3 us
  Pallas kernels  39.6 us (98%)
  between operations  0.64 us (2%)
    pallas_call x1, Pallas kernels, local(): pl.pallas_call(kernel, out_shape=(jax.ShapeDtypeStruct((SEGS, ROW), BF),...  38.7 us
    pallas_call x1, Pallas kernels, local(): pl.pallas_call(store, out_shape=(jax.ShapeDtypeStruct((SEGS, ROW), BF), j...  0.9 us

profile of v5, /device:TPU:1, one launch (start us, length us, event | category | flops | bytes accessed | tf_op | source)
XLA Modules:
  0.0 40.3 jit_solution(13179706561570559726)
XLA Ops:
  0.6 38.7 %shard_map.104 = (bf16[1024,128]{1,0:T(8,128)(2,1)S(1)}, bf16[2048,128]{1,0:T(8,128)(2,1)S(1)}) custom-call(s32[8,128]{1,0:T(8,128)} %bitcast.2, s32[8,128]{1,0:T(8,128)} %bitcast.3, f32[8,128]{1,0:T(8,128)} %constant.2.clone.place_hbm, bf16[64,64]{1,0:T(8,128)(2,1)} %d_hbm.1, bf16[64,64]{1,0:T(8,128)(2,1)} %m_hbm.1, bf16[128,128]{1,0:T(8,128)(2,1)} %conduct_hbm.1, ...), custom_call_target="tpu_custom_call" | custom-call | flops 8589934592 | bytes 2097152 | tf_op jit(solution)/shard_map/pallas_call | solution.py:397
  39.4 0.9 %shard_map.105 = (bf16[1024,128]{1,0:T(8,128)(2,1)}, bf16[2048,128]{1,0:T(8,128)(2,1)}) custom-call(bf16[1024,128]{1,0:T(8,128)(2,1)S(1)} %get-tuple-element.4.cast_in, bf16[2048,128]{1,0:T(8,128)(2,1)S(1)} %get-tuple-element.5.mold_in), custom_call_target="tpu_custom_call" | custom-call | tf_op jit(solution)/shard_map/pallas_call | solution.py:461

commit v6 on v5

--- a/solution.py
+++ b/solution.py
@@ -36,7 +36,7 @@
     rest = offsets[1:]
     def key(o):
         dz, dy, dc, dx = o
-        return ((dc - dz & 1) * 4 + (dx - dz - dy & 3)) * 16 + dz * 4 + dy
+        return ((dc - dz & 1) * 4 + [0,2,1,3].index(dx - dz - dy & 3)) * 16 + [0,1,2,3].index(dz) * 4 + [0,1,2,3].index(dy)
     rest.sort(key=key)
     return offsets[:1] + rest
 
@@ -66,7 +66,8 @@
     mold_hbm,
     volume_hbm,
     cout_v,
-    mout_v,
+    rest_v,
+    placed_out,
     owner_ref,
     face_ref,
     place_ref,
@@ -84,7 +85,7 @@
     ids_recv,
     wgap_v,
     mfour_v,
-    wcond_v,
+    cond_v,
     tile_v,
     spread_v,
     row8_v,
@@ -250,10 +251,7 @@
     mfour_v[...] = jnp.zeros_like(mfour_v)
     mfour_v[NODES:, 0:ROW] = mtwo
     mfour_v[NODES:, ROW:] = mtwo
-    for half in range(2):
-        pick = jnp.where((down == lane + half * NODES) & (lane < NODES), 0.5, 0.0)
-        wcond_v[half, 0:ROW, :] = pick.astype(BF)
-        wcond_v[half, ROW:, :] = (conduct_ref[...].astype(F32) * -0.5).astype(BF)
+    cond_v[...] = (conduct_ref[...].astype(F32) * -0.5).astype(BF)
     wide_d, wide_l = iota((ROW, SLOTS), 0), iota((ROW, SLOTS), 1)
     tile = jnp.where(wide_d == (wide_l & 31), 1.0, jnp.where(wide_d == (wide_l & 31) + 64, 256.0, 0.0))
     tile_v[...] = tile.astype(BF)
@@ -359,34 +357,41 @@
         acc_v[...] += jnp.dot(pick, back_v[span].reshape(SLOTS, ROW), preferred_element_type=F32)
         return 0
 
-    lax.fori_loop(0, BATCHES - 2, collect, 0)
-
-    lax.fori_loop(BATCHES - 2, BATCHES, collect, 0)
+    loads[3].wait()
+
+    def cool(n, _):
+        rows = pl.ds(pl.multiple_of(n * 256, 256), 256)
+        volume = volume_v[rows, :]
+        rest_v[rows, :] = volume.astype(F32) + jnp.dot(volume, cond_v[...], preferred_element_type=F32)
+        return 0
+
+    lax.fori_loop(0, FACES // 256, cool, 0)
+    lax.fori_loop(0, BATCHES, collect, 0)
     cout_v[...] = acc_v[...].astype(BF)
-    loads[3].wait()
     wait_for(placed_v, tot_sem.at[0])
-    for u in range(4):
-        for half in range(2):
-            rows = slice(u * QUARTER + half * 256, u * QUARTER + half * 256 + 256)
-            volume = volume_v[rows, :]
-            both = jnp.concatenate([placed_v[u], volume], axis=1)
-            change = jnp.dot(both, wcond_v[half], preferred_element_type=F32)
-            mout_v[rows, :] = (volume.astype(F32) + change).astype(BF)
-
+    placed_out[...] = placed_v[...]
     wait_for(ids_send.at[pl.ds(1, PEERS - 1)], sent_sem.at[0])
     wait_for(send_v.at[pl.ds(1, PEERS - 1)], sent_sem.at[1])
     wait_for(ans_v.at[pl.ds(1, PEERS - 1)], sent_sem.at[2])
     wait_for(quarter_v.at[pl.ds(0, 3)], sent_sem.at[3])
 
 
-def store(cast_in, mold_in, cast_out, mold_out, sem):
-    copies = [
-        pltpu.make_async_copy(cast_in, cast_out, sem.at[0]),
-        pltpu.make_async_copy(mold_in, mold_out, sem.at[1]),
+def finish(cast_in, rest_in, placed_in, cast_out, mold_out, mold_v, sem):
+    stores = [pltpu.make_async_copy(cast_in, cast_out, sem.at[0])]
+    stores[0].start()
+    down, lane = iota((ROW, ROW), 0), iota((ROW, ROW), 1)
+    pick = [
+        jnp.where((down == lane + half * NODES) & (lane < NODES), 0.5, 0.0).astype(BF) for half in range(2)
     ]
-    for copy in copies:
-        copy.start()
-    for copy in copies:
+    for n in range(FACES // 256):
+        rows = pl.ds(n * 256, 256)
+        heat = jnp.dot(placed_in[n // 2], pick[n % 2], preferred_element_type=F32)
+        mold_v[rows, :] = (rest_in[rows, :] + heat).astype(BF)
+        if n % 2:
+            rows = pl.ds((n - 1) * 256, 512)
+            stores.append(pltpu.make_async_copy(mold_v.at[rows], mold_out.at[rows], sem.at[len(stores)]))
+            stores[-1].start()
+    for copy in stores:
         copy.wait()
 
 
@@ -398,10 +403,11 @@
         kernel,
         out_shape=(
             jax.ShapeDtypeStruct((SEGS, ROW), BF),
-            jax.ShapeDtypeStruct((FACES, ROW), BF),
+            jax.ShapeDtypeStruct((FACES, ROW), F32),
+            jax.ShapeDtypeStruct((4, 256, ROW), BF),
         ),
         in_specs=[hbm] * 9,
-        out_specs=(vmem, vmem),
+        out_specs=(vmem, vmem, vmem),
         scratch_shapes=[
             pltpu.VMEM((8, ROW), I32),
             pltpu.VMEM((8, ROW), I32),
@@ -420,7 +426,7 @@
             pltpu.VMEM((PEERS, ROW), F32),
             pltpu.VMEM((ROW, 2 * ROW), BF),
             pltpu.VMEM((ROW, 2 * ROW), BF),
-            pltpu.VMEM((2, 2 * ROW, ROW), BF),
+            pltpu.VMEM((ROW, ROW), BF),
             pltpu.VMEM((ROW, SLOTS), BF),
             pltpu.VMEM((ROW, 2 * ROW), BF),
             pltpu.VMEM((8, ROW), F32),
@@ -459,14 +465,14 @@
         )
     )
     return pl.pallas_call(
-        store,
+        finish,
         out_shape=(
             jax.ShapeDtypeStruct((SEGS, ROW), BF),
             jax.ShapeDtypeStruct((FACES, ROW), BF),
         ),
-        in_specs=[vmem] * 2,
+        in_specs=[vmem] * 3,
         out_specs=(hbm, hbm),
-        scratch_shapes=[pltpu.SemaphoreType.DMA((2,))],
+        scratch_shapes=[pltpu.VMEM((FACES, ROW), BF), pltpu.SemaphoreType.DMA((5,))],
     )(*(pltpu.with_memory_space_constraint(a, pltpu.VMEM) for a in made))
 
 

time: 40.4 us -> 39.9 us (0.988)
    pallas_call x1, Pallas kernels: 38.7 us -> 38.2 us  [local(): pl.pallas_call(kernel, out_shape=(jax.ShapeDtypeStruct((SEGS, ROW), BF),...]
where the time goes in v6:
time: 39.9 us; the launch traced here: 39.8 us
  Pallas kernels  39.2 us (98%)
  between operations  0.64 us (2%)
    pallas_call x1, Pallas kernels, local(): pl.pallas_call(kernel, out_shape=(jax.ShapeDtypeStruct((SEGS, ROW), BF),...  38.2 us
    pallas_call x1, Pallas kernels, local(): pl.pallas_call(finish, out_shape=(jax.ShapeDtypeStruct((SEGS, ROW), BF),...  1.02 us

profile of v6, /device:TPU:1, one launch (start us, length us, event | category | flops | bytes accessed | tf_op | source)
XLA Modules:
  0.0 39.8 jit_solution(8022860789523772722)
XLA Ops:
  0.6 38.2 %shard_map.104 = (bf16[1024,128]{1,0:T(8,128)(2,1)S(1)}, f32[2048,128]{1,0:T(8,128)S(1)}, bf16[4,256,128]{2,1,0:T(8,128)(2,1)S(1)}) custom-call(s32[8,128]{1,0:T(8,128)} %bitcast.2, s32[8,128]{1,0:T(8,128)} %bitcast.3, f32[8,128]{1,0:T(8,128)} %constant.2.clone.place_hbm, bf16[64,64]{1,0:T(8,128)(2,1)} %d_hbm.1, bf16[64,64]{1,0:T(8,128)(2,1)} %m_hbm.1, ...), custom_call_target="tpu_custom_call" | custom-call | flops 8589934592 | bytes 2097152 | tf_op jit(solution)/shard_map/pallas_call | solution.py:402
  38.8 1.0 %shard_map.105 = (bf16[1024,128]{1,0:T(8,128)(2,1)}, bf16[2048,128]{1,0:T(8,128)(2,1)}) custom-call(bf16[1024,128]{1,0:T(8,128)(2,1)S(1)} %get-tuple-element.5.cast_in, f32[2048,128]{1,0:T(8,128)S(1)} %get-tuple-element.6.rest_in, bf16[4,256,128]{2,1,0:T(8,128)(2,1)S(1)} %get-tuple-element.7.placed_in), custom_call_target="tpu_custom_call" | custom-call | tf_op jit(solution)/shard_map/pallas_call | solution.py:467
